TPU v7x, 32 devices: a whole 2x2x4 slice. The times are simulated.
32 devices in a mesh: groups: 2 (over y), expert: 16 (over z, x, core).
Axes of the slice: x: 2, y: 2, z: 4, core: 2. Of those that a mesh axis runs over, the one named last changes fastest.
Arguments:
- tokens: bfloat16 [1024, 2048], P(('groups', 'expert')), parts along dimension 0, may hold values from -6 to 6
- grad_out: bfloat16 [1024, 2048], P(('groups', 'expert')), parts along dimension 0, may hold values from -6 to 6
- route_prob: float32 [1024], P(('groups', 'expert')), parts along dimension 0, may hold values from 0.25 to 1
- block_expert: int32 [256], P(('groups', 'expert')), parts along dimension 0, may hold values from 0 to 15, as said below
- block_live: int32 [256], P(('groups', 'expert')), parts along dimension 0, may hold values from 2 to 4, as said below
- expert_weights: bfloat16 [16, 3, 2048, 384], P('expert'), may hold values from -0.1875 to 0.1875
Outputs:
- d_tokens: bfloat16 [1024, 2048], P(('groups', 'expert')), parts along dimension 0
- d_prob: float32 [1024], P(('groups', 'expert')), parts along dimension 0
- weight_grads: bfloat16 [32, 3, 2048, 384], P(('groups', 'expert')), parts along dimension 0
There are 2 independent parts, one for each index of `groups`. A program takes and returns all parts, laid end to end along the dimension named above; an argument that names none is the same for every part. Nothing has to cross between parts.
Inputs may be any that keep to these rules, and one draw needn't show every extreme that they name: `block_expert`: on each device the 8 blocks name, in an order drawn per device, exactly one of the two experts e and e + 8 for every e below 8. Every expert is named by 1 to 15 blocks in all, and one expert by exactly 15. `block_live`: some block has 4 live rows and some has 2.
All inputs are finite; a program needn't handle non-finite values.
Results may differ from a plain program's by a relative error of at most 0.0061.
Values may be sent and summed in bfloat16 or wider, within the bound.
A program may use at most 128 MiB of HBM per device.

v0:
```python
import jax
import jax.numpy as jnp
from jax import lax
from jax.sharding import PartitionSpec as P


def expert_rows(inputs, cotangent, weights):
    gate_proj = jnp.dot(inputs, weights[0], preferred_element_type=jnp.float32)
    up_proj = jnp.dot(inputs, weights[1], preferred_element_type=jnp.float32)
    sigma = jax.nn.sigmoid(gate_proj)
    active = gate_proj * sigma
    hidden = (active * up_proj).astype(jnp.bfloat16)
    produced = jnp.dot(hidden, weights[2].T, preferred_element_type=jnp.float32).astype(
        jnp.bfloat16
    )
    pulled = jnp.dot(cotangent, weights[2], preferred_element_type=jnp.float32)
    d_gate = (pulled * up_proj * sigma * (1.0 + gate_proj * (1.0 - sigma))).astype(jnp.bfloat16)
    d_up = (pulled * active).astype(jnp.bfloat16)
    d_input = (
        jnp.dot(d_gate, weights[0].T, preferred_element_type=jnp.float32)
        + jnp.dot(d_up, weights[1].T, preferred_element_type=jnp.float32)
    ).astype(jnp.bfloat16)
    return (hidden, produced, d_gate, d_up, d_input)


def weight_terms(inputs, cotangent, hidden, d_gate, d_up):
    return jnp.stack(
        [
            jnp.dot(inputs.T, d_gate, preferred_element_type=jnp.float32),
            jnp.dot(inputs.T, d_up, preferred_element_type=jnp.float32),
            jnp.dot(cotangent.T, hidden, preferred_element_type=jnp.float32),
        ]
    )


def add_slots(buffer, values, start):
    present = lax.dynamic_slice_in_dim(buffer, start, values.shape[0], 0)
    return lax.dynamic_update_slice_in_dim(buffer, present + values, start, 0)


def shards(tokens, grad_out, route_prob, block_expert, block_live, expert_weights):
    axis_size = lax.axis_size("expert")
    device = lax.axis_index("expert")
    half_size = axis_size // 2
    blocks_here = block_expert.shape[0]
    width = tokens.shape[1]
    block_rows = tokens.shape[0] // blocks_here
    tile_slots = min(64 // block_rows, half_size)
    within = jnp.arange(block_rows, dtype=jnp.int32)
    live_rows = within[None, :] < block_live[:, None]
    inputs = jnp.where(live_rows[:, :, None], tokens.reshape(blocks_here, block_rows, width), 0)
    scaled = route_prob.reshape(blocks_here, block_rows)[:, :, None] * grad_out.reshape(
        blocks_here, block_rows, width
    ).astype(jnp.float32)
    cotangent = jnp.where(live_rows[:, :, None], scaled, 0.0).astype(jnp.bfloat16)
    far_side = (device - block_expert) % axis_size >= half_size
    block_kind = far_side.astype(jnp.int32)
    own_weights = expert_weights[0]
    slot_ids = jnp.arange(axis_size, dtype=jnp.int32)
    matches = block_expert[None, :] == slot_ids[:, None]
    occupied = jnp.any(matches, axis=1)
    source_block = jnp.sum(
        jnp.where(matches, jnp.arange(blocks_here, dtype=jnp.int32)[None, :], 0), axis=1
    )
    send_inputs = jnp.where(occupied[:, None, None], jnp.take(inputs, source_block, axis=0), 0)
    send_cotangent = jnp.where(
        occupied[:, None, None], jnp.take(cotangent, source_block, axis=0), 0
    )
    send_kind = jnp.where(occupied, jnp.take(block_kind, source_block), 2)
    got_inputs, got_cotangent, got_kind = (
        lax.all_to_all(send_inputs, "expert", split_axis=0, concat_axis=0, tiled=True),
        lax.all_to_all(send_cotangent, "expert", split_axis=0, concat_axis=0, tiled=True),
        lax.all_to_all(send_kind, "expert", split_axis=0, concat_axis=0, tiled=True),
    )
    arrival = jnp.argsort(got_kind * axis_size + slot_ids)
    own_count = jnp.sum((got_kind == 0).astype(jnp.int32))
    far_count = jnp.sum((got_kind == 1).astype(jnp.int32))
    sorted_inputs = jnp.take(got_inputs, arrival, axis=0)
    sorted_cotangent = jnp.take(got_cotangent, arrival, axis=0)

    def run_tiles(first_slot, last_slot, weights, state):
        tiles_needed = (last_slot - first_slot + tile_slots - 1) // tile_slots

        def one_tile(tile_index, carried):
            produced_all, d_input_all, grad_sum = carried
            start = first_slot + tile_index * tile_slots
            keep = start + jnp.arange(tile_slots, dtype=jnp.int32) < last_slot
            piece_in = jnp.where(
                keep[:, None, None],
                lax.dynamic_slice_in_dim(sorted_inputs, start, tile_slots, 0),
                0,
            ).reshape(-1, width)
            piece_cot = jnp.where(
                keep[:, None, None],
                lax.dynamic_slice_in_dim(sorted_cotangent, start, tile_slots, 0),
                0,
            ).reshape(-1, width)
            hidden, produced, d_gate, d_up, d_input = expert_rows(piece_in, piece_cot, weights)
            grad_sum = grad_sum + weight_terms(piece_in, piece_cot, hidden, d_gate, d_up)
            produced_all = add_slots(
                produced_all, produced.reshape(tile_slots, block_rows, width), start
            )
            d_input_all = add_slots(
                d_input_all, d_input.reshape(tile_slots, block_rows, width), start
            )
            return (produced_all, d_input_all, grad_sum)

        return lax.fori_loop(0, tiles_needed, one_tile, state)

    zero_slots = jnp.zeros((axis_size, block_rows, width), jnp.bfloat16)
    zero_grads = jnp.zeros((3,) + own_weights.shape[1:], jnp.float32)
    produced_all, d_input_all, near_grads = run_tiles(
        0, own_count, own_weights, (zero_slots, zero_slots, zero_grads)
    )
    produced_all, d_input_all, far_grads = run_tiles(
        own_count, own_count + far_count, own_weights, (produced_all, d_input_all, zero_grads)
    )
    inverse = jnp.argsort(arrival)
    back_produced = jnp.take(produced_all, inverse, axis=0)
    back_d_input = jnp.take(d_input_all, inverse, axis=0)
    ret_produced, ret_d_input = (
        lax.all_to_all(back_produced, "expert", split_axis=0, concat_axis=0, tiled=True),
        lax.all_to_all(back_d_input, "expert", split_axis=0, concat_axis=0, tiled=True),
    )
    mine_produced = jnp.take(ret_produced, block_expert, axis=0).reshape(-1, width)
    mine_d_input = jnp.take(ret_d_input, block_expert, axis=0).reshape(-1, width)
    d_prob = jnp.sum(grad_out.astype(jnp.float32) * mine_produced.astype(jnp.float32), axis=1)
    far_rounded = far_grads.astype(jnp.bfloat16)
    far_home = lax.optimization_barrier(far_rounded)
    weight_grads = (near_grads + far_home.astype(jnp.float32)).astype(jnp.bfloat16)[None]
    return (mine_d_input, d_prob, weight_grads)


def solution(mesh):
    placed = (
        P(("groups", "expert"), None),
        P(("groups", "expert"), None),
        P(("groups", "expert")),
        P(("groups", "expert")),
        P(("groups", "expert")),
        P("expert", None, None, None),
    )
    return jax.shard_map(
        shards,
        mesh=mesh,
        in_specs=placed,
        out_specs=(
            P(("groups", "expert"), None),
            P(("groups", "expert")),
            P(("groups", "expert"), None, None, None),
        ),
        check_vma=False,
    )
```

profile of v0, /device:TPU:0, one launch (start us, length us, event | category | flops | bytes accessed | tf_op | source)
XLA Modules:
  0.0 136.8 jit_solution(1470267622418513870)
XLA Ops:
  2.1 1.2 compare_and_fusion
  4.7 7.4 %all-to-all-start = ((s32[16,1,1]{2,1,0:T(1,128)}), s32[16,1,1]{2,1,0:T(1,128)S(1)}, u32[]{:S(2)}, u32[]{:S(2)}) async-start(s32[16,1,1]{2,1,0:T(1,128)} %copy.13), calls=%async_computation | async-start | bytes 16384 | tf_op jit(solution)/shard_map/all_to_all | solution.py:73
  17.4 1.2 select_select_fusion
  18.6 6.0 %all-to-all-start.2 = ((bf16[16,4,2048]{2,1,0:T(4,128)(2,1)}), bf16[16,4,2048]{2,1,0:T(4,128)(2,1)S(1)}, u32[]{:S(2)}, u32[]{:S(2)}) async-start(bf16[16,4,2048]{2,1,0:T(4,128)(2,1)} %get-tuple-element.318), calls=%async_computation.2 | async-start | bytes 524288 | tf_op jit(solution)/shard_map/all_to_all | solution.py:72
  25.5 1.2 sort.31
  26.8 1.2 sort.32
  28.7 5.9 %all-to-all-done.2 = bf16[16,4,2048]{2,1,0:T(4,128)(2,1)S(1)} async-done(((bf16[16,4,2048]{2,1,0:T(4,128)(2,1)}), bf16[16,4,2048]{2,1,0:T(4,128)(2,1)S(1)}, u32[]{:S(2)}, u32[]{:S(2)}) %all-to-all-start.2) | async-done | bytes 262176 | tf_op jit(solution)/shard_map/all_to_all | solution.py:72
  34.6 3.5 %all-to-all-start.1 = ((bf16[16,4,2048]{2,1,0:T(4,128)(2,1)}), bf16[16,4,2048]{2,1,0:T(4,128)(2,1)S(1)}, u32[]{:S(2)}, u32[]{:S(2)}) async-start(bf16[16,4,2048]{2,1,0:T(4,128)(2,1)} %get-tuple-element.319), calls=%async_computation.1 | async-start | bytes 524288 | tf_op jit(solution)/shard_map/all_to_all | solution.py:71
  42.7 5.5 %all-to-all-done.1 = bf16[16,4,2048]{2,1,0:T(4,128)(2,1)S(1)} async-done(((bf16[16,4,2048]{2,1,0:T(4,128)(2,1)}), bf16[16,4,2048]{2,1,0:T(4,128)(2,1)S(1)}, u32[]{:S(2)}, u32[]{:S(2)}) %all-to-all-start.1) | async-done | bytes 262176 | tf_op jit(solution)/shard_map/all_to_all | solution.py:71
  49.5 4.2 %broadcast_in_dim.146.clone = f32[3,2048,384]{2,1,0:T(8,128)} broadcast(f32[]{:T(128)} %constant.151.clone.1), dimensions={} | broadcast | bytes 9437188 | tf_op jit(solution)/shard_map/broadcast_in_dim | solution.py:111
  53.7 23.3 %while.32 = (s32[]{:T(128)}, bf16[16,4,2048]{2,1,0:T(4,128)(2,1)S(1)}, bf16[16,4,2048]{2,1,0:T(4,128)(2,1)S(1)}, f32[3,2048,384]{2,1,0:T(8,128)}, s32[]{:T(128)}...) while((s32[]{:T(128)}, ...), condition=%wide.region_5.8_spmd, body=%wide.region_4.7_spmd.sunk | while | flops 461099008 | bytes 51536080 | solution.py:108
  54.6 1.7 %fusion.125 = f32[32,384]{1,0:T(8,128)S(1)} fusion(bf16[32,2048]{1,0:T(8,128)(2,1)S(1)} %reshape.288, bf16[3,2048,384]{2,1,0:T(8,128)(2,1)} %get-tuple-element.507), kind=kOutput, calls=%fused_computation.24.clone.1 | convolution fusion | flops 50331648 | bytes 1753088 | tf_op jit(solution)/shard_map/while/body/dot_general | solution.py:8
  56.4 1.7 %fusion.126 = f32[32,384]{1,0:T(8,128)S(1)} fusion(bf16[32,2048]{1,0:T(8,128)(2,1)S(1)} %reshape.288, bf16[3,2048,384]{2,1,0:T(8,128)(2,1)} %get-tuple-element.507), kind=kOutput, calls=%fused_computation.20.clone.1 | convolution fusion | flops 50331648 | bytes 1753088 | tf_op jit(solution)/shard_map/while/body/dot_general | solution.py:9
  58.2 1.8 %multiply_convert_fusion.8 = (bf16[32,384]{1,0:T(8,128)(2,1)S(1)}, bf16[32,384]{1,0:T(8,128)(2,1)S(1)}, bf16[32,384]{1,0:T(8,128)(2,1)S(1)}) fusion(f32[32,384]{1,0:T(8,128)S(1)} %fusion.125, f32[32,384]{1,0:T(8,128)S(1)} %fusion.126, bf16[32,2048]{1,0:T(8,128)(2,1)S(1)} %reshape.289, bf16[3,2048,384]{2,1,0:T(8,128)(2,1)} %get-tuple-element.507), kind=kOutput, calls=%fused_computation.36.clone.1 | convolution fusion | flops 50515968 | bytes 1875968 | tf_op jit(solution)/shard_map/while/body/dot_general | solution.py:16
  59.9 2.0 %fusion.127 = f32[32,2048]{1,0:T(8,128)S(1)} fusion(bf16[32,384]{1,0:T(8,128)(2,1)S(1)} %get-tuple-element.452, bf16[3,2048,384]{2,1,0:T(8,128)(2,1)} %get-tuple-element.507), kind=kOutput, calls=%fused_computation.22.clone.1 | convolution fusion | flops 50331648 | bytes 1859584 | tf_op jit(solution)/shard_map/while/body/dot_general | solution.py:20
  61.9 2.0 %fusion.128 = bf16[32,2048]{1,0:T(8,128)(2,1)S(1)} fusion(f32[32,2048]{1,0:T(8,128)S(1)} %fusion.127, bf16[32,384]{1,0:T(8,128)(2,1)S(1)} %get-tuple-element.453, bf16[3,2048,384]{2,1,0:T(8,128)(2,1)} %get-tuple-element.507), kind=kOutput, calls=%fused_computation.14.clone.1 | convolution fusion | flops 50462720 | bytes 1990656 | tf_op jit(solution)/shard_map/while/body/dot_general | solution.py:21
  64.0 2.0 %convolution_convert_fusion.4 = bf16[32,2048]{1,0:T(8,128)(2,1)S(1)} fusion(bf16[32,384]{1,0:T(8,128)(2,1)S(1)} %get-tuple-element.454, bf16[3,2048,384]{2,1,0:T(8,128)(2,1)} %get-tuple-element.507), kind=kOutput, calls=%fused_computation.15.clone.1 | convolution fusion | flops 50397184 | bytes 1728512 | tf_op jit(solution)/shard_map/while/body/dot_general | solution.py:13
  68.1 8.9 %maximum_add_fusion.4 = f32[3,2048,384]{2,1,0:T(8,128)} fusion(f32[3,2048,384]{2,1,0:T(8,128)} %get-tuple-element.490, f32[1,2048,384]{2,1,0:T(8,128)S(1)} %convolution_bitcast_fusion.12, f32[1,2048,384]{2,1,0:T(8,128)S(1)} %convolution_bitcast_fusion.13, f32[1,2048,384]{2,1,0:T(8,128)S(1)} %convolution_bitcast_fusion.14), kind=kLoop, calls=%fused_computation.9.clone.1 | loop fusion | flops 7077888 | bytes 28311552 | tf_op jit(solution)/shard_map/while/body/add | solution.py:99
  77.0 4.3 %broadcast_in_dim.146 = f32[3,2048,384]{2,1,0:T(8,128)} broadcast(f32[]{:T(128)} %constant.151.clone.1), dimensions={} | broadcast | bytes 9437188 | tf_op jit(solution)/shard_map/broadcast_in_dim | solution.py:111
  81.2 23.2 %while.33 = (s32[]{:T(128)}, bf16[16,4,2048]{2,1,0:T(4,128)(2,1)S(1)}, bf16[16,4,2048]{2,1,0:T(4,128)(2,1)S(1)}, f32[3,2048,384]{2,1,0:T(8,128)}, s32[]{:T(128)}...) while((s32[]{:T(128)}, ...), condition=%wide.region_8.11_spmd, body=%wide.region_7.10_spmd.sunk | while | flops 461099040 | bytes 51536104 | solution.py:108
  82.2 1.7 %fusion.146 = f32[32,384]{1,0:T(8,128)S(1)} fusion(bf16[32,2048]{1,0:T(8,128)(2,1)S(1)} %reshape.292, bf16[3,2048,384]{2,1,0:T(8,128)(2,1)} %get-tuple-element.549), kind=kOutput, calls=%fused_computation.57.clone.1 | convolution fusion | flops 50331648 | bytes 1753088 | tf_op jit(solution)/shard_map/while/body/dot_general | solution.py:8
  83.9 1.7 %fusion.147 = f32[32,384]{1,0:T(8,128)S(1)} fusion(bf16[32,2048]{1,0:T(8,128)(2,1)S(1)} %reshape.292, bf16[3,2048,384]{2,1,0:T(8,128)(2,1)} %get-tuple-element.549), kind=kOutput, calls=%fused_computation.53.clone.1 | convolution fusion | flops 50331648 | bytes 1753088 | tf_op jit(solution)/shard_map/while/body/dot_general | solution.py:9
  85.7 1.8 %multiply_convert_fusion.9 = (bf16[32,384]{1,0:T(8,128)(2,1)S(1)}, bf16[32,384]{1,0:T(8,128)(2,1)S(1)}, bf16[32,384]{1,0:T(8,128)(2,1)S(1)}) fusion(f32[32,384]{1,0:T(8,128)S(1)} %fusion.146, f32[32,384]{1,0:T(8,128)S(1)} %fusion.147, bf16[32,2048]{1,0:T(8,128)(2,1)S(1)} %reshape.293, bf16[3,2048,384]{2,1,0:T(8,128)(2,1)} %get-tuple-element.549), kind=kOutput, calls=%fused_computation.69.clone.1 | convolution fusion | flops 50515968 | bytes 1875968 | tf_op jit(solution)/shard_map/while/body/dot_general | solution.py:16
  87.5 2.0 %fusion.148 = f32[32,2048]{1,0:T(8,128)S(1)} fusion(bf16[32,384]{1,0:T(8,128)(2,1)S(1)} %get-tuple-element.469, bf16[3,2048,384]{2,1,0:T(8,128)(2,1)} %get-tuple-element.549), kind=kOutput, calls=%fused_computation.55.clone.1 | convolution fusion | flops 50331648 | bytes 1859584 | tf_op jit(solution)/shard_map/while/body/dot_general | solution.py:20
  89.5 2.0 %fusion.149 = bf16[32,2048]{1,0:T(8,128)(2,1)S(1)} fusion(f32[32,2048]{1,0:T(8,128)S(1)} %fusion.148, bf16[32,384]{1,0:T(8,128)(2,1)S(1)} %get-tuple-element.470, bf16[3,2048,384]{2,1,0:T(8,128)(2,1)} %get-tuple-element.549), kind=kOutput, calls=%fused_computation.47.clone.1 | convolution fusion | flops 50462720 | bytes 1990656 | tf_op jit(solution)/shard_map/while/body/dot_general | solution.py:21
  91.5 2.0 %convolution_convert_fusion.5 = bf16[32,2048]{1,0:T(8,128)(2,1)S(1)} fusion(bf16[32,384]{1,0:T(8,128)(2,1)S(1)} %get-tuple-element.471, bf16[3,2048,384]{2,1,0:T(8,128)(2,1)} %get-tuple-element.549), kind=kOutput, calls=%fused_computation.48.clone.1 | convolution fusion | flops 50397184 | bytes 1728512 | tf_op jit(solution)/shard_map/while/body/dot_general | solution.py:13
  95.6 8.8 %maximum_add_fusion.5 = f32[3,2048,384]{2,1,0:T(8,128)} fusion(f32[3,2048,384]{2,1,0:T(8,128)} %get-tuple-element.530, f32[1,2048,384]{2,1,0:T(8,128)S(1)} %convolution_bitcast_fusion.15, f32[1,2048,384]{2,1,0:T(8,128)S(1)} %convolution_bitcast_fusion.16, f32[1,2048,384]{2,1,0:T(8,128)S(1)} %convolution_bitcast_fusion.17), kind=kLoop, calls=%fused_computation.42.clone.1 | loop fusion | flops 7077888 | bytes 28311552 | tf_op jit(solution)/shard_map/while/body/add | solution.py:99
  107.4 3.5 %all-to-all-start.4 = ((bf16[16,4,2048]{2,1,0:T(4,128)(2,1)}), bf16[16,4,2048]{2,1,0:T(4,128)(2,1)S(1)}, u32[]{:S(2)}, u32[]{:S(2)}) async-start(bf16[16,4,2048]{2,1,0:T(4,128)(2,1)} %get-tuple-element.322), calls=%async_computation.4 | async-start | bytes 524288 | tf_op jit(solution)/shard_map/all_to_all | solution.py:122
  110.9 6.4 %convert_element_type.121 = bf16[3,2048,384]{2,1,0:T(8,128)(2,1)} convert(f32[3,2048,384]{2,1,0:T(8,128)} %get-tuple-element.263) | non-fusion elementwise | flops 2359296 | bytes 14155776 | tf_op jit(solution)/shard_map/convert_element_type | solution.py:128
  117.3 3.6 %all-to-all-done.4 = bf16[16,4,2048]{2,1,0:T(4,128)(2,1)S(1)} async-done(((bf16[16,4,2048]{2,1,0:T(4,128)(2,1)}), bf16[16,4,2048]{2,1,0:T(4,128)(2,1)S(1)}, u32[]{:S(2)}, u32[]{:S(2)}) %all-to-all-start.4) | async-done | bytes 262176 | tf_op jit(solution)/shard_map/all_to_all | solution.py:122
  120.9 3.5 %all-to-all-start.3 = ((bf16[16,4,2048]{2,1,0:T(4,128)(2,1)}), bf16[16,4,2048]{2,1,0:T(4,128)(2,1)S(1)}, u32[]{:S(2)}, u32[]{:S(2)}) async-start(bf16[16,4,2048]{2,1,0:T(4,128)(2,1)} %get-tuple-element.323), calls=%async_computation.3 | async-start | bytes 524288 | tf_op jit(solution)/shard_map/all_to_all | solution.py:123
  124.5 8.2 %fusion.36 = bf16[1,3,2048,384]{3,2,1,0:T(8,128)(2,1)} fusion(f32[3,2048,384]{2,1,0:T(8,128)} %get-tuple-element.262, bf16[3,2048,384]{2,1,0:T(8,128)(2,1)} %convert_element_type.121), kind=kLoop, calls=%fused_computation.76 | loop fusion | flops 7077888 | bytes 18874368 | tf_op jit(solution)/shard_map/broadcast_in_dim | solution.py:130
  (76 shorter events, 25.3 us)
Async XLA Ops:
  4.7 13.9 %all-to-all-start = ((s32[16,1,1]{2,1,0:T(1,128)}), s32[16,1,1]{2,1,0:T(1,128)S(1)}, u32[]{:S(2)}, u32[]{:S(2)}) async-start(s32[16,1,1]{2,1,0:T(1,128)} %copy.13), calls=%async_computation | async-start | bytes 16384 | tf_op jit(solution)/shard_map/all_to_all | solution.py:73
  18.6 16.1 %all-to-all-start.2 = ((bf16[16,4,2048]{2,1,0:T(4,128)(2,1)}), bf16[16,4,2048]{2,1,0:T(4,128)(2,1)S(1)}, u32[]{:S(2)}, u32[]{:S(2)}) async-start(bf16[16,4,2048]{2,1,0:T(4,128)(2,1)} %get-tuple-element.318), calls=%async_computation.2 | async-start | bytes 524288 | tf_op jit(solution)/shard_map/all_to_all | solution.py:72
  34.6 13.5 %all-to-all-start.1 = ((bf16[16,4,2048]{2,1,0:T(4,128)(2,1)}), bf16[16,4,2048]{2,1,0:T(4,128)(2,1)S(1)}, u32[]{:S(2)}, u32[]{:S(2)}) async-start(bf16[16,4,2048]{2,1,0:T(4,128)(2,1)} %get-tuple-element.319), calls=%async_computation.1 | async-start | bytes 524288 | tf_op jit(solution)/shard_map/all_to_all | solution.py:71
  81.2 25.0 %copy-start.2 = (pred[16]{0:T(512)(128)(4,1)S(1)}, pred[16]{0:T(512)(128)(4,1)}, u32[]{:S(2)}) copy-start(pred[16]{0:T(512)(128)(4,1)} %compare_and_fusion.1) | copy-start | bytes 52
  81.2 29.7 %copy-start.3 = (s32[8]{0:T(128)S(1)}, s32[8]{0:T(128)}, u32[]{:S(2)}) copy-start(s32[8]{0:T(128)} %param.19) | copy-start | bytes 100
  107.4 13.5 %all-to-all-start.4 = ((bf16[16,4,2048]{2,1,0:T(4,128)(2,1)}), bf16[16,4,2048]{2,1,0:T(4,128)(2,1)S(1)}, u32[]{:S(2)}, u32[]{:S(2)}) async-start(bf16[16,4,2048]{2,1,0:T(4,128)(2,1)} %get-tuple-element.322), calls=%async_computation.4 | async-start | bytes 524288 | tf_op jit(solution)/shard_map/all_to_all | solution.py:122
  120.9 13.5 %all-to-all-start.3 = ((bf16[16,4,2048]{2,1,0:T(4,128)(2,1)}), bf16[16,4,2048]{2,1,0:T(4,128)(2,1)S(1)}, u32[]{:S(2)}, u32[]{:S(2)}) async-start(bf16[16,4,2048]{2,1,0:T(4,128)(2,1)} %get-tuple-element.323), calls=%async_computation.3 | async-start | bytes 524288 | tf_op jit(solution)/shard_map/all_to_all | solution.py:123
  124.4 10.7 %copy-start.1 = (pred[8]{0:T(512)(128)(4,1)S(1)}, pred[8]{0:T(512)(128)(4,1)}, u32[]{:S(2)}) copy-start(pred[8]{0:T(512)(128)(4,1)} %get-tuple-element.324) | copy-start | bytes 28
  124.5 11.6 %copy-start = (bf16[32,2048]{1,0:T(8,128)(2,1)S(1)}, bf16[32,2048]{1,0:T(8,128)(2,1)}, u32[]{:S(2)}) copy-start(bf16[32,2048]{1,0:T(8,128)(2,1)} %param.17) | copy-start | bytes 393220
where the time goes:
time: 138 us; the launch traced here: 137 us
  other arithmetic  46.1 us (33%)
  matrix products  26.1 us (19%)
  starting transfers between devices  24 us (17%)
  local copies, waits for them, and re-layouts  20.2 us (15%)
  waiting for transfers between devices  16.1 us (12%)
  between operations  3.45 us (2%)
    add x2, other arithmetic, one_tile(): grad_sum + weight_terms(piece_in, piece_cot, hidden, d_gate, d_up)  17.7 us
    broadcast_in_dim x2, local copies, waits for them, and re-layouts, shards(): zero_grads = jnp.zeros((3,) + own_weights.shape[1:], jnp.float32)  8.5 us
    broadcast_in_dim x1, other arithmetic, shards(): (near_grads + far_home.astype(jnp.float32)).astype(jnp.bfloat16)[None]  8.21 us
    all_to_all x1, starting transfers between devices, shards(): lax.all_to_all(send_kind, 'expert', split_axis=0, concat_axis=0, tiled=True)  7.36 us
    convert_element_type x1, other arithmetic, shards(): far_rounded = far_grads.astype(jnp.bfloat16)  6.37 us
    all_to_all x1, starting transfers between devices, shards(): lax.all_to_all(send_cotangent, 'expert', split_axis=0, concat_axis=0, til...  6.01 us
    all_to_all x1, waiting for transfers between devices, shards(): lax.all_to_all(send_cotangent, 'expert', split_axis=0, concat_axis=0, til...  5.92 us
    all_to_all x1, waiting for transfers between devices, shards(): lax.all_to_all(send_inputs, 'expert', split_axis=0, concat_axis=0, tiled=...  5.5 us
  transfers between devices with their start and end apart: 5, of which 4 were waited for; matrix products, arithmetic and copies ran while one was open for 20% of the time, Pallas kernels for 0%

commit v1 on v0

v1 whole, which is shorter than its diff:
```python
import functools

import jax
import jax.numpy as jnp
from jax import lax
from jax.experimental import pallas as pl
from jax.experimental.pallas import tpu as pltpu
from jax.sharding import PartitionSpec as P

MESH = pl.DeviceIdType.MESH
SLOT = 16
F32 = jnp.float32
BF16 = jnp.bfloat16


def dot(a, b):
    return jnp.dot(a, b, preferred_element_type=F32)


def dot_nt(a, b):
    return lax.dot_general(a, b, (((1,), (1,)), ((), ())), preferred_element_type=F32)


def dot_tn(a, b):
    return lax.dot_general(a, b, (((0,), (0,)), ((), ())), preferred_element_type=F32)


def kernel(
    n, blk, group,
    tok_hbm, go_hbm, prob_hbm, be_hbm, live_hbm, w_ref,
    dtok_ref, dprob_ref, wg_ref,
    tok_ref, go_ref, prob_ref, be_ref, live_ref, wcat, wdown, send_x, send_c, got_x, got_c, send_d, got_d, send_t, got_t,
    rows_x, rows_c, d_cat, hid,
    in_sem, w_sem, sx_sem, rx_sem, sc_sem, rc_sem, sd_sem, rd_sem, st_sem, rt_sem,
):
    me = lax.axis_index("expert")
    rows, width = tok_ref.shape
    ff = wdown.shape[1]
    nblk = rows // blk
    parts = SLOT // blk
    pw = width // parts
    cols = parts * rows
    span = group * SLOT
    grow = group * blk
    lanes = prob_ref.shape[1]

    half = n // 2
    side = me // half * half
    place = me % half

    def others(body):
        def across(k, carry):
            body(half - side + (place + k) % half)
            return carry

        def beside(k, carry):
            body(side + (place + k) % half)
            return carry

        lax.fori_loop(0, half, across, 0)
        lax.fori_loop(1, half, beside, 0)

    def slot(ref, i):
        return ref.at[pl.ds(pl.multiple_of(i * SLOT, SLOT), SLOT), :]

    def remote(src, dst, ssem, rsem, to):
        return pltpu.make_async_remote_copy(
            src_ref=src, dst_ref=dst, send_sem=ssem, recv_sem=rsem,
            device_id={"expert": to}, device_id_type=MESH,
        )

    def send(src, dst, ssem, rsem):
        others(lambda to: remote(slot(src, to), slot(dst, me), ssem, rsem, to).start())

    def every_slot(src, dst, ssem, rsem):
        part = pl.ds(0, (n - 1) * SLOT)
        return remote(src.at[part, :], dst.at[part, :], ssem, rsem, (me + 1) % n)

    barrier = pltpu.get_barrier_semaphore()
    others(
        lambda to: pl.semaphore_signal(
            barrier, inc=1, device_id={"expert": to}, device_id_type=MESH
        )
    )
    inputs = [
        pltpu.make_async_copy(src, dst, in_sem.at[j])
        for j, (src, dst) in enumerate(
            (
                (be_hbm, be_ref), (live_hbm, live_ref), (prob_hbm, prob_ref),
                (tok_hbm, tok_ref), (go_hbm, go_ref),
            )
        )
    ]
    for load in inputs:
        load.start()
    loads = [
        pltpu.make_async_copy(w_ref.at[0, 0], wcat.at[:, pl.ds(0, ff)], w_sem.at[0]),
        pltpu.make_async_copy(w_ref.at[0, 1], wcat.at[:, pl.ds(ff, ff)], w_sem.at[1]),
        pltpu.make_async_copy(w_ref.at[0, 2], wdown, w_sem.at[2]),
    ]
    for load in loads:
        load.start()
    for load in inputs:
        load.wait()

    def keys(shape, axis):
        k = lax.broadcasted_iota(jnp.int32, shape, axis)
        part, row = k // rows, k % rows
        block, within = row // blk, row % blk
        owner = jnp.zeros(shape, jnp.int32)
        live = jnp.zeros(shape, jnp.int32)
        for b in range(nblk):
            owner = jnp.where(block == b, be_ref[b], owner)
            live = jnp.where(block == b, live_ref[b], live)
        return jnp.where(within < live, owner * SLOT + part * blk + within, -1)

    def stacked(value):
        return jnp.concatenate([value[:, p * pw:(p + 1) * pw] for p in range(parts)], axis=0)

    def one_hot(mask):
        return jnp.where(mask, 1.0, 0.0).astype(BF16)

    probs = []
    for g in range(rows // lanes):
        square = (lanes, lanes)
        diagonal = lax.broadcasted_iota(jnp.int32, square, 0) == lax.broadcasted_iota(
            jnp.int32, square, 1
        )
        line = jnp.broadcast_to(prob_ref[g:g + 1, :], square)
        probs.append(jnp.sum(jnp.where(diagonal, line, 0.0), axis=1, keepdims=True))
    prob = jnp.concatenate(probs, axis=0) if len(probs) > 1 else probs[0]
    tok4 = stacked(tok_ref[...])
    cot4 = stacked((prob * go_ref[...].astype(F32)).astype(BF16))
    key_row = keys((1, cols), 1)

    def pack(c, carry):
        at = pl.multiple_of(c * span, span)
        ids = lax.broadcasted_iota(jnp.int32, (span, cols), 0) + c * span
        pick = one_hot(ids == key_row)
        send_x[pl.ds(at, span), :] = dot(pick, tok4).astype(BF16)
        send_c[pl.ds(at, span), :] = dot(pick, cot4).astype(BF16)
        return carry

    lax.fori_loop(0, n // group, pack, 0)
    pl.semaphore_wait(barrier, n - 1)
    send(send_x, got_x, sx_sem, rx_sem)
    send(send_c, got_c, sc_sem, rc_sem)
    slot(got_x, me)[...] = slot(send_x, me)[...]
    slot(got_c, me)[...] = slot(send_c, me)[...]

    i = lax.broadcasted_iota(jnp.int32, (span, span), 0)
    k = lax.broadcasted_iota(jnp.int32, (span, span), 1)
    unslot = one_hot(k == ((i % grow) // blk) * SLOT + (i // grow) * blk + i % blk)
    toslot = one_hot(i == ((k % grow) // blk) * SLOT + (k // grow) * blk + k % blk)

    def unpack(got, into):
        def step(c, carry):
            at = pl.multiple_of(c * span, span)
            out = pl.multiple_of(c * grow, grow)
            value = dot(unslot, got[pl.ds(at, span), :]).astype(BF16)
            for p in range(parts):
                into[pl.ds(out, grow), p * pw:(p + 1) * pw] = value[p * grow:(p + 1) * grow, :]
            return carry

        lax.fori_loop(0, n // group, step, 0)

    every_slot(send_x, got_x, sx_sem, rx_sem).wait_recv()
    unpack(got_x, rows_x)
    for load in loads:
        load.wait()

    def forward(c, carry):
        out = pl.multiple_of(c * grow, grow)
        d_cat[pl.ds(out, grow), :] = dot(rows_x[pl.ds(out, grow), :], wcat[...])
        return carry

    lax.fori_loop(0, n // group, forward, 0)
    every_slot(send_c, got_c, sc_sem, rc_sem).wait_recv()
    unpack(got_c, rows_c)

    def backward(c, carry):
        out = pl.multiple_of(c * grow, grow)
        here = pl.ds(out, grow)
        gate, up = d_cat[here, :ff], d_cat[here, ff:]
        pulled = dot(rows_c[here, :], wdown[...])
        sigma = jax.nn.sigmoid(gate)
        active = gate * sigma
        hidden = (active * up).astype(BF16)
        hid[here, :] = hidden
        share = jnp.sum(hidden.astype(F32) * pulled, axis=1, keepdims=True)
        share = jnp.broadcast_to(share, (grow, send_t.shape[2]))
        for j in range(group):
            send_t[c * group + j] = share[j * blk:(j + 1) * blk, :]
        d_cat[here, :ff] = pulled * up * sigma * (1.0 + gate * (1.0 - sigma))
        d_cat[here, ff:] = pulled * active
        return carry

    lax.fori_loop(0, n // group, backward, 0)

    others(lambda to: remote(send_t.at[to], got_t.at[me], st_sem, rt_sem, to).start())
    every_t = remote(
        send_t.at[pl.ds(0, n - 1)], got_t.at[pl.ds(0, n - 1)], st_sem, rt_sem, (me + 1) % n
    )
    got_t[me] = send_t[me]

    def rows_back(c, carry):
        at = pl.multiple_of(c * span, span)
        here = pl.ds(pl.multiple_of(c * grow, grow), grow)
        d_in = dot_nt(d_cat[here, :].astype(BF16), wcat[...]).astype(BF16)
        send_d[pl.ds(at, span), :] = dot(toslot, stacked(d_in)).astype(BF16)
        return carry

    lax.fori_loop(0, n // group, rows_back, 0)
    send(send_d, got_d, sd_sem, rd_sem)
    slot(got_d, me)[...] = slot(send_d, me)[...]

    d_all = d_cat[...].astype(BF16)
    for p in range(parts):
        here = pl.ds(p * pw, pw)
        grads = dot_tn(rows_x[:, here], d_all).astype(BF16)
        wg_ref[0, 0, here, :] = grads[:, :ff]
        wg_ref[0, 1, here, :] = grads[:, ff:]
        wg_ref[0, 2, here, :] = dot_tn(rows_c[:, here], hid[...]).astype(BF16)

    every_t.wait_recv()
    lane = lax.broadcasted_iota(jnp.int32, (blk, got_t.shape[2]), 1)
    row = lax.broadcasted_iota(jnp.int32, (blk, got_t.shape[2]), 0)
    per = lanes // blk
    for g in range(rows // lanes):
        line = jnp.zeros((blk, got_t.shape[2]), F32)
        for j in range(per):
            line = jnp.where(lane == j * blk + row, got_t[be_ref[g * per + j]], line)
        total = jnp.sum(line, axis=0, keepdims=True)[:, :lanes]
        dprob_ref[g:g + 1, :] = total / prob_ref[g:g + 1, :]

    key_column = keys((cols, 1), 0)
    every_slot(send_d, got_d, sd_sem, rd_sem).wait_recv()

    def home(c, total):
        at = pl.multiple_of(c * span, span)
        ids = lax.broadcasted_iota(jnp.int32, (cols, span), 1) + c * span
        return total + dot(one_hot(ids == key_column), got_d[pl.ds(at, span), :])

    total = home(0, jnp.zeros((cols, pw), F32))
    if n // group > 1:
        total = lax.fori_loop(1, n // group, home, total)
    for p in range(parts):
        dtok_ref[:, p * pw:(p + 1) * pw] = total[p * rows:(p + 1) * rows, :].astype(BF16)

    every_slot(send_x, got_x, sx_sem, rx_sem).wait_send()
    every_slot(send_c, got_c, sc_sem, rc_sem).wait_send()
    every_slot(send_d, got_d, sd_sem, rd_sem).wait_send()
    every_t.wait_send()


def store_kernel(*refs):
    count = len(refs) // 2
    sems = refs[-1]
    stores = [
        pltpu.make_async_copy(src, dst, sems.at[j])
        for j, (src, dst) in enumerate(zip(refs[:count], refs[count:2 * count]))
    ]
    for store in stores:
        store.start()
    for store in stores:
        store.wait()


def shards(n, tokens, grad_out, route_prob, block_expert, block_live, expert_weights):
    rows, width = tokens.shape
    blk = rows // block_expert.shape[0]
    ff = expert_weights.shape[3]
    parts = SLOT // blk
    pw = width // parts
    group = min(n, 16)
    lanes = min(rows, 128)
    slots = (n * SLOT, pw)
    every = n * blk
    vmem = pl.BlockSpec(memory_space=pltpu.VMEM)
    any_ = pl.BlockSpec(memory_space=pl.ANY)
    dma = pltpu.SemaphoreType.DMA
    shapes = (
        ((rows, width), BF16),
        ((rows // lanes, lanes), F32),
        ((1, 3, width, ff), BF16),
    )
    results = pl.pallas_call(
        functools.partial(kernel, n, blk, group),
        out_shape=tuple(pltpu.VMEM(*shape) for shape in shapes),
        in_specs=[any_] * 6,
        out_specs=(vmem,) * 3,
        scratch_shapes=[
            pltpu.VMEM((rows, width), BF16),
            pltpu.VMEM((rows, width), BF16),
            pltpu.VMEM((rows // lanes, lanes), F32),
            pltpu.SMEM(block_expert.shape, jnp.int32),
            pltpu.SMEM(block_live.shape, jnp.int32),
            pltpu.VMEM((width, 2 * ff), BF16),
            pltpu.VMEM((width, ff), BF16),
            *[pltpu.VMEM(slots, BF16) for _ in range(6)],
            *[pltpu.VMEM((n, blk, 128), F32) for _ in range(2)],
            pltpu.VMEM((every, width), BF16),
            pltpu.VMEM((every, width), BF16),
            pltpu.VMEM((every, 2 * ff), F32),
            pltpu.VMEM((every, ff), BF16),
            dma((5,)),
            dma((3,)),
            *[dma for _ in range(8)],
        ],
        compiler_params=pltpu.CompilerParams(
            collective_id=0, has_side_effects=True, vmem_limit_bytes=52 * 1024 * 1024
        ),
        cost_estimate=pl.CostEstimate(
            flops=2 * every * width * ff * 8,
            bytes_accessed=2 * 3 * width * ff * 2,
            transcendentals=every * ff,
        ),
    )(
        *[
            pltpu.with_memory_space_constraint(value, pltpu.HBM)
            for value in (
                tokens, grad_out, route_prob.reshape(rows // lanes, lanes),
                block_expert, block_live, expert_weights,
            )
        ]
    )
    d_tokens, d_prob, weight_grads = pl.pallas_call(
        store_kernel,
        out_shape=tuple(jax.ShapeDtypeStruct(*shape) for shape in shapes),
        in_specs=[vmem] * 3,
        out_specs=(any_,) * 3,
        scratch_shapes=[dma((3,))],
        compiler_params=pltpu.CompilerParams(vmem_limit_bytes=1024 * 1024),
    )(*results)
    return (d_tokens, d_prob.reshape(rows), weight_grads)


def solution(mesh):
    placed = (
        P(("groups", "expert"), None),
        P(("groups", "expert"), None),
        P(("groups", "expert")),
        P(("groups", "expert")),
        P(("groups", "expert")),
        P("expert", None, None, None),
    )
    return jax.shard_map(
        functools.partial(shards, mesh.shape["expert"]),
        mesh=mesh,
        in_specs=placed,
        out_specs=(
            P(("groups", "expert"), None),
            P(("groups", "expert")),
            P(("groups", "expert"), None, None, None),
        ),
        check_vma=False,
    )
```

time: 138 us -> 32.7 us (0.24)
  other arithmetic: 46.1 us -> 0 us
  Pallas kernels: 0 us -> 32 us
  matrix products: 26.1 us -> 0 us
  starting transfers between devices: 24 us -> 0 us
  local copies, waits for them, and re-layouts: 20.2 us -> 0 us
  waiting for transfers between devices: 16.1 us -> 0 us
  between operations: 3.45 us -> 0.64 us
    pallas_call x0 -> x2, Pallas kernels: none -> 32 us  [the longest x1 29.7 us: shards(): pl.pallas_call(functools.partial(kernel, n, blk, group), out_shape=tuple(...]
    dot_general x18 -> x0, matrix products: 26.1 us -> none  [the longest x2 4.02 us: expert_rows(): jnp.dot(d_up, weights[1].T, preferred_element_type=jnp.float32)]
    all_to_all x5 -> x0, starting transfers between devices: 24 us -> none  [the longest x1 7.36 us: shards(): lax.all_to_all(send_kind, 'expert', split_axis=0, concat_axis=0, tiled=True)]
    add x3 -> x0, other arithmetic: 17.7 us -> none  [the longest x2 17.7 us: one_tile(): grad_sum + weight_terms(piece_in, piece_cot, hidden, d_gate, d_up)]
    all_to_all x5 -> x0, waiting for transfers between devices: 16.1 us -> none  [the longest x1 5.92 us: shards(): lax.all_to_all(send_cotangent, 'expert', split_axis=0, concat_axis=0, til...]
    broadcast_in_dim x4 -> x0, local copies, waits for them, and re-layouts: 8.69 us -> none  [the longest x2 8.5 us: shards(): zero_grads = jnp.zeros((3,) + own_weights.shape[1:], jnp.float32)]
    broadcast_in_dim x1 -> x0, other arithmetic: 8.21 us -> none  [shards(): (near_grads + far_home.astype(jnp.float32)).astype(jnp.bfloat16)[None]]
    gather x9 -> x0, local copies, waits for them, and re-layouts: 6.82 us -> none  [the longest x1 0.89 us: shards(): back_d_input = jnp.take(d_input_all, inverse, axis=0)]
  transfers between devices with their start and end apart: 5 -> 0, of which waited for: 4 -> 0; matrix products, arithmetic and copies ran while one was open for 20% -> 0% of each run, Pallas kernels for 0% -> 0%
where the time goes in v1:
time: 32.7 us; the launch traced here: 32.6 us
  Pallas kernels  32 us (98%)
  between operations  0.64 us (2%)
    pallas_call x1, Pallas kernels, shards(): pl.pallas_call(functools.partial(kernel, n, blk, group), out_shape=tuple(...  29.7 us
    pallas_call x1, Pallas kernels, shards(): pl.pallas_call(store_kernel, out_shape=tuple((jax.ShapeDtypeStruct(*shape...  2.26 us

profile of v1, /device:TPU:0, one launch (start us, length us, event | category | flops | bytes accessed | tf_op | source)
XLA Modules:
  0.0 32.6 jit_solution(10597982488994284283)
XLA Ops:
  0.6 29.7 %shard_map.85 = (bf16[32,2048]{1,0:T(8,128)(2,1)S(1)}, f32[1,32]{1,0:T(1,128)S(1)}, bf16[1,3,2048,384]{3,2,1,0:T(8,128)(2,1)S(1)}) custom-call(bf16[32,2048]{1,0:T(8,128)(2,1)} %tok_hbm.1, bf16[32,2048]{1,0:T(8,128)(2,1)} %go_hbm.1, f32[1,32]{1,0:T(1,128)} %bitcast.2, s32[8]{0:T(128)} %be_hbm.1, s32[8]{0:T(128)} %live_hbm.1, bf16[1,3,2048,384]{3,2,1,0:T(8,128)(2,1)} %w_ref.1), custom_call_target="tpu_custom_call" | custom-call | flops 805306368 | bytes 9437184 | tf_op jit(solution)/shard_map/pallas_call | solution.py:287
  30.3 2.3 %shard_map.86 = (bf16[32,2048]{1,0:T(8,128)(2,1)}, f32[1,32]{1,0:T(1,128)}, bf16[1,3,2048,384]{3,2,1,0:T(8,128)(2,1)}) custom-call(bf16[32,2048]{1,0:T(8,128)(2,1)S(1)} %get-tuple-element.9.refs_0_, f32[1,32]{1,0:T(1,128)S(1)} %get-tuple-element.10.refs_1_, bf16[1,3,2048,384]{3,2,1,0:T(8,128)(2,1)S(1)} %get-tuple-element.11.refs_2_), custom_call_target="tpu_custom_call" | custom-call | tf_op jit(solution)/shard_map/pallas_call | solution.py:327

commit v2 on v1

v2 whole, which is shorter than its diff:
```python
import functools

import jax
import jax.numpy as jnp
from jax import lax
from jax.experimental import pallas as pl
from jax.experimental.pallas import tpu as pltpu
from jax.sharding import PartitionSpec as P

MESH = pl.DeviceIdType.MESH
SLOT = 16
F32 = jnp.float32
BF16 = jnp.bfloat16


def dot(a, b):
    return jnp.dot(a, b, preferred_element_type=F32)


def dot_nt(a, b):
    return lax.dot_general(a, b, (((1,), (1,)), ((), ())), preferred_element_type=F32)


def dot_tn(a, b):
    return lax.dot_general(a, b, (((0,), (0,)), ((), ())), preferred_element_type=F32)


def kernel(
    n, blk, group,
    tok_hbm, go_hbm, prob_hbm, be_hbm, live_hbm, w_ref,
    got_d, back_ref, dprob_ref, wg_ref,
    tok_ref, go_ref, prob_ref, be_ref, live_ref, wcat, wdown,
    send_x, send_c, got_x, got_c, send_d, send_t, got_t, rows_x, rows_c, d_cat, hid,
    in_sem, w_sem, sx_sem, rx_sem, sc_sem, rc_sem, sd_sem, rd_sem, st_sem, rt_sem,
):
    me = lax.axis_index("expert")
    rows, width = tok_ref.shape
    ff = wdown.shape[1]
    nblk = rows // blk
    parts = SLOT // blk
    pw = width // parts
    cols = parts * rows
    lanes = prob_ref.shape[1]
    half = n // 2
    mid = half + half // 2
    side = me // half * half
    place = me % half

    def ahead(k):
        base = jnp.where(k < half, side, half - side)
        return base + (place + k) % half

    def behind(k):
        base = jnp.where(k < half, side, half - side)
        return base + (place - k + n) % half

    def slots(first, last, body):
        def step(k, carry):
            body(k)
            return carry

        lax.fori_loop(first, last, step, 0)

    def part_of(ref, first, count):
        if len(ref.shape) == 3:
            return ref.at[pl.ds(first, count)]
        start = first * SLOT
        if not isinstance(first, int):
            start = pl.multiple_of(start, SLOT)
        return ref.at[pl.ds(start, count * SLOT), :]

    def remote(src, dst, ssem, rsem, to, first, count):
        return pltpu.make_async_remote_copy(
            src_ref=part_of(src, first, count), dst_ref=part_of(dst, first, count),
            send_sem=ssem, recv_sem=rsem,
            device_id={"expert": to}, device_id_type=MESH,
        )

    def send(first, last, src, dst, ssem, rsem, where):
        slots(first, last, lambda k: remote(src, dst, ssem, rsem, where(k), k, 1).start())

    def whole(first, last, src, dst, ssem, rsem):
        return remote(src, dst, ssem, rsem, ahead(1), first, last - first)

    barrier = pltpu.get_barrier_semaphore()
    slots(
        1, n,
        lambda k: pl.semaphore_signal(
            barrier, inc=1, device_id={"expert": ahead(k)}, device_id_type=MESH
        ),
    )
    inputs = [
        pltpu.make_async_copy(src, dst, in_sem.at[j])
        for j, (src, dst) in enumerate(
            (
                (be_hbm, be_ref), (live_hbm, live_ref), (tok_hbm, tok_ref),
                (prob_hbm, prob_ref), (go_hbm, go_ref),
            )
        )
    ]
    for load in inputs:
        load.start()
    loads = [
        pltpu.make_async_copy(w_ref.at[0, 0], wcat.at[:, pl.ds(0, ff)], w_sem.at[0]),
        pltpu.make_async_copy(w_ref.at[0, 1], wcat.at[:, pl.ds(ff, ff)], w_sem.at[1]),
        pltpu.make_async_copy(w_ref.at[0, 2], wdown, w_sem.at[2]),
    ]
    for load in loads:
        load.start()

    def slot_of(expert):
        return (expert % half - place + half) % half + jnp.where(
            expert // half * half == side, 0, half
        )

    def keys(shape, axis):
        k = lax.broadcasted_iota(jnp.int32, shape, axis)
        part, row = k // rows, k % rows
        block, within = row // blk, row % blk
        owner = jnp.zeros(shape, jnp.int32)
        live = jnp.zeros(shape, jnp.int32)
        for b in range(nblk):
            owner = jnp.where(block == b, slot_of(be_ref[b]), owner)
            live = jnp.where(block == b, live_ref[b], live)
        return jnp.where(within < live, owner * SLOT + part * blk + within, -1)

    def stacked(value):
        return jnp.concatenate([value[:, p * pw:(p + 1) * pw] for p in range(parts)], axis=0)

    def one_hot(mask):
        return jnp.where(mask, 1.0, 0.0).astype(BF16)

    bulk = min(n, 16) * SLOT

    def pack(value, into):
        def step(c, carry):
            at = pl.multiple_of(c * bulk, bulk)
            ids = lax.broadcasted_iota(jnp.int32, (bulk, cols), 0) + c * bulk
            into[pl.ds(at, bulk), :] = dot(one_hot(ids == key_row), value).astype(BF16)
            return carry

        lax.fori_loop(0, n * SLOT // bulk, step, 0)

    for load in inputs[:3]:
        load.wait()
    key_row = keys((1, cols), 1)
    pack(stacked(tok_ref[...]), send_x)
    pl.semaphore_wait(barrier, n - 1)
    send(half, mid, send_x, got_x, sx_sem.at[0], rx_sem.at[0], ahead)
    send(1, half, send_x, got_x, sx_sem.at[0], rx_sem.at[0], ahead)

    for load in inputs[3:]:
        load.wait()
    probs = []
    for g in range(rows // lanes):
        square = (lanes, lanes)
        diagonal = lax.broadcasted_iota(jnp.int32, square, 0) == lax.broadcasted_iota(
            jnp.int32, square, 1
        )
        line = jnp.broadcast_to(prob_ref[g:g + 1, :], square)
        probs.append(jnp.sum(jnp.where(diagonal, line, 0.0), axis=1, keepdims=True))
    prob = jnp.concatenate(probs, axis=0) if len(probs) > 1 else probs[0]
    pack(stacked((prob * go_ref[...].astype(F32)).astype(BF16)), send_c)
    send(half, mid, send_c, got_c, sc_sem.at[0], rc_sem.at[0], ahead)
    send(1, half, send_c, got_c, sc_sem.at[0], rc_sem.at[0], ahead)
    send(mid, n, send_x, got_x, sx_sem.at[1], rx_sem.at[1], ahead)
    send(mid, n, send_c, got_c, sc_sem.at[1], rc_sem.at[1], ahead)
    got_x[:SLOT, :] = send_x[:SLOT, :]
    got_c[:SLOT, :] = send_c[:SLOT, :]

    key_column = keys((cols, 1), 0)

    def pick_back(c, carry):
        at = pl.multiple_of(c * bulk, bulk)
        ids = lax.broadcasted_iota(jnp.int32, (cols, bulk), 1) + c * bulk
        back_ref[:, pl.ds(at, bulk)] = one_hot(ids == key_column)
        return carry

    lax.fori_loop(0, n * SLOT // bulk, pick_back, 0)

    class Chunk:
        def __init__(self, first, last, count):
            self.first, self.last, self.count = first, last, count
            self.span, self.grow = count * SLOT, count * blk
            i = lax.broadcasted_iota(jnp.int32, (self.span, self.span), 0)
            k = lax.broadcasted_iota(jnp.int32, (self.span, self.span), 1)
            grow = self.grow
            self.unslot = one_hot(k == (i % grow) // blk * SLOT + i // grow * blk + i % blk)
            self.toslot = one_hot(i == (k % grow) // blk * SLOT + k // grow * blk + k % blk)

        def each(self, body):
            def step(c, carry):
                first = self.first + c * self.count
                body(
                    first,
                    pl.ds(pl.multiple_of(first * SLOT, SLOT), self.span),
                    pl.ds(pl.multiple_of(first * blk, SLOT), self.grow),
                )
                return carry

            lax.fori_loop(0, (self.last - self.first) // self.count, step, 0)

        def unpack(self, got, into):
            def body(first, slot_rows, here):
                value = dot(self.unslot, got[slot_rows, :]).astype(BF16)
                for p in range(parts):
                    into[here, p * pw:(p + 1) * pw] = value[p * self.grow:(p + 1) * self.grow, :]

            self.each(body)

        def forward(self):
            def body(first, slot_rows, here):
                d_cat[here, :] = dot(rows_x[here, :], wcat[...])

            self.each(body)

        def backward(self):
            def body(first, slot_rows, here):
                gate, up = d_cat[here, :ff], d_cat[here, ff:]
                pulled = dot(rows_c[here, :], wdown[...])
                sigma = jax.nn.sigmoid(gate)
                active = gate * sigma
                hidden = (active * up).astype(BF16)
                hid[here, :] = hidden
                share = jnp.sum(hidden.astype(F32) * pulled, axis=1, keepdims=True)
                share = jnp.broadcast_to(share, (self.grow, send_t.shape[2]))
                for j in range(self.count):
                    send_t[first + j] = share[j * blk:(j + 1) * blk, :]
                d_cat[here, :ff] = pulled * up * sigma * (1.0 + gate * (1.0 - sigma))
                d_cat[here, ff:] = pulled * active
                d_in = dot_nt(d_cat[here, :].astype(BF16), wcat[...]).astype(BF16)
                send_d[slot_rows, :] = dot(self.toslot, stacked(d_in)).astype(BF16)

            self.each(body)

    early, late = Chunk(0, mid, 3 * group), Chunk(mid, n, group)
    whole(1, mid, send_x, got_x, sx_sem.at[0], rx_sem.at[0]).wait_recv()
    early.unpack(got_x, rows_x)
    for load in loads:
        load.wait()
    early.forward()
    whole(1, mid, send_c, got_c, sc_sem.at[0], rc_sem.at[0]).wait_recv()
    early.unpack(got_c, rows_c)
    early.backward()
    send(1, half, send_d, got_d, sd_sem, rd_sem, behind)
    got_d[:SLOT, :] = send_d[:SLOT, :]
    whole(mid, n, send_x, got_x, sx_sem.at[1], rx_sem.at[1]).wait_recv()
    late.unpack(got_x, rows_x)
    late.forward()
    whole(mid, n, send_c, got_c, sc_sem.at[1], rc_sem.at[1]).wait_recv()
    send(half, mid, send_d, got_d, sd_sem, rd_sem, behind)
    late.unpack(got_c, rows_c)
    late.backward()
    send(mid, n, send_d, got_d, sd_sem, rd_sem, behind)
    send(1, n, send_t, got_t, st_sem, rt_sem, behind)
    got_t[0] = send_t[0]

    d_all = d_cat[...].astype(BF16)
    for p in range(parts):
        here = pl.ds(p * pw, pw)
        grads = dot_tn(rows_x[:, here], d_all).astype(BF16)
        wg_ref[0, 0, here, :] = grads[:, :ff]
        wg_ref[0, 1, here, :] = grads[:, ff:]
        wg_ref[0, 2, here, :] = dot_tn(rows_c[:, here], hid[...]).astype(BF16)

    every_t = whole(1, n, send_t, got_t, st_sem, rt_sem)
    every_t.wait_recv()
    lane = lax.broadcasted_iota(jnp.int32, (blk, got_t.shape[2]), 1)
    row = lax.broadcasted_iota(jnp.int32, (blk, got_t.shape[2]), 0)
    per = lanes // blk
    for g in range(rows // lanes):
        line = jnp.zeros((blk, got_t.shape[2]), F32)
        for j in range(per):
            line = jnp.where(lane == j * blk + row, got_t[slot_of(be_ref[g * per + j])], line)
        total = jnp.sum(line, axis=0, keepdims=True)[:, :lanes]
        dprob_ref[g:g + 1, :] = total / prob_ref[g:g + 1, :]

    for j, (first, last) in enumerate(((1, mid), (mid, n))):
        whole(first, last, send_x, got_x, sx_sem.at[j], rx_sem.at[j]).wait_send()
        whole(first, last, send_c, got_c, sc_sem.at[j], rc_sem.at[j]).wait_send()
    every_t.wait_send()
    every_d = whole(1, n, send_d, got_d, sd_sem, rd_sem)
    every_d.wait_send()
    every_d.wait_recv()


def store_kernel(got_d, back, d_prob, wg, dtok_hbm, dprob_hbm, wg_hbm, d_tokens, sem):
    stores = [
        pltpu.make_async_copy(wg, wg_hbm, sem.at[0]),
        pltpu.make_async_copy(d_prob, dprob_hbm, sem.at[1]),
        pltpu.make_async_copy(d_tokens, dtok_hbm, sem.at[2]),
    ]
    stores[0].start()
    stores[1].start()
    rows = d_tokens.shape[0]
    pw = got_d.shape[1]
    parts = d_tokens.shape[1] // pw
    for p in range(parts):
        picked = dot(back[p * rows:(p + 1) * rows, :], got_d[...])
        d_tokens[:, p * pw:(p + 1) * pw] = picked.astype(BF16)
    stores[2].start()
    for store in stores:
        store.wait()


def shards(n, tokens, grad_out, route_prob, block_expert, block_live, expert_weights):
    rows, width = tokens.shape
    blk = rows // block_expert.shape[0]
    ff = expert_weights.shape[3]
    parts = SLOT // blk
    pw = width // parts
    group = min(n // 4, 4)
    lanes = min(rows, 128)
    slots = (n * SLOT, pw)
    every = n * blk
    vmem = pl.BlockSpec(memory_space=pltpu.VMEM)
    any_ = pl.BlockSpec(memory_space=pl.ANY)
    dma = pltpu.SemaphoreType.DMA
    shapes = (
        ((rows, width), BF16),
        ((rows // lanes, lanes), F32),
        ((1, 3, width, ff), BF16),
    )
    results = pl.pallas_call(
        functools.partial(kernel, n, blk, group),
        out_shape=(
            pltpu.VMEM(slots, BF16),
            pltpu.VMEM((parts * rows, n * SLOT), BF16),
            *[pltpu.VMEM(*shape) for shape in shapes[1:]],
        ),
        in_specs=[any_] * 6,
        out_specs=(vmem,) * 4,
        scratch_shapes=[
            pltpu.VMEM((rows, width), BF16),
            pltpu.VMEM((rows, width), BF16),
            pltpu.VMEM((rows // lanes, lanes), F32),
            pltpu.SMEM(block_expert.shape, jnp.int32),
            pltpu.SMEM(block_live.shape, jnp.int32),
            pltpu.VMEM((width, 2 * ff), BF16),
            pltpu.VMEM((width, ff), BF16),
            *[pltpu.VMEM(slots, BF16) for _ in range(5)],
            *[pltpu.VMEM((n, blk, 128), F32) for _ in range(2)],
            pltpu.VMEM((every, width), BF16),
            pltpu.VMEM((every, width), BF16),
            pltpu.VMEM((every, 2 * ff), F32),
            pltpu.VMEM((every, ff), BF16),
            dma((5,)),
            dma((3,)),
            *[dma((2,)) for _ in range(4)],
            *[dma for _ in range(4)],
        ],
        compiler_params=pltpu.CompilerParams(
            collective_id=0, has_side_effects=True, vmem_limit_bytes=40 * 1024 * 1024
        ),
        cost_estimate=pl.CostEstimate(
            flops=2 * every * width * ff * 8,
            bytes_accessed=2 * 3 * width * ff * 2,
            transcendentals=every * ff,
        ),
    )(
        *[
            pltpu.with_memory_space_constraint(value, pltpu.HBM)
            for value in (
                tokens, grad_out, route_prob.reshape(rows // lanes, lanes),
                block_expert, block_live, expert_weights,
            )
        ]
    )
    d_tokens, d_prob, weight_grads = pl.pallas_call(
        store_kernel,
        out_shape=tuple(jax.ShapeDtypeStruct(*shape) for shape in shapes),
        in_specs=[vmem] * 4,
        out_specs=(any_,) * 3,
        scratch_shapes=[pltpu.VMEM((rows, width), BF16), dma((3,))],
        compiler_params=pltpu.CompilerParams(vmem_limit_bytes=8 * 1024 * 1024),
    )(*results)
    return (d_tokens, d_prob.reshape(rows), weight_grads)


def solution(mesh):
    placed = (
        P(("groups", "expert"), None),
        P(("groups", "expert"), None),
        P(("groups", "expert")),
        P(("groups", "expert")),
        P(("groups", "expert")),
        P("expert", None, None, None),
    )
    return jax.shard_map(
        functools.partial(shards, mesh.shape["expert"]),
        mesh=mesh,
        in_specs=placed,
        out_specs=(
            P(("groups", "expert"), None),
            P(("groups", "expert")),
            P(("groups", "expert"), None, None, None),
        ),
        check_vma=False,
    )
```

time: 32.7 us -> 31.1 us (0.951)
  Pallas kernels: 32 us -> 30.3 us
    pallas_call x1, Pallas kernels: 29.7 us -> 28.1 us  [shards(): pl.pallas_call(functools.partial(kernel, n, blk, group), out_shape=(pltpu...]
where the time goes in v2:
time: 31.1 us; the launch traced here: 31 us
  Pallas kernels  30.3 us (97%)
  between operations  0.64 us (2%)
    pallas_call x1, Pallas kernels, shards(): pl.pallas_call(functools.partial(kernel, n, blk, group), out_shape=(pltpu...  28.1 us
    pallas_call x1, Pallas kernels, shards(): pl.pallas_call(store_kernel, out_shape=tuple((jax.ShapeDtypeStruct(*shape...  2.25 us

profile of v2, /device:TPU:0, one launch (start us, length us, event | category | flops | bytes accessed | tf_op | source)
XLA Modules:
  0.0 31.0 jit_solution(4717637136322053209)
XLA Ops:
  0.6 28.1 %shard_map.85 = (bf16[256,512]{1,0:T(8,128)(2,1)S(1)}, bf16[128,256]{1,0:T(8,128)(2,1)S(1)}, f32[1,32]{1,0:T(1,128)S(1)}, bf16[1,3,2048,384]{3,2,1,0:T(8,128)(2,1)S(1)}) custom-call(bf16[32,2048]{1,0:T(8,128)(2,1)} %tok_hbm.1, bf16[32,2048]{1,0:T(8,128)(2,1)} %go_hbm.1, f32[1,32]{1,0:T(1,128)} %bitcast.2, s32[8]{0:T(128)} %be_hbm.1, s32[8]{0:T(128)} %live_hbm.1, ...), custom_call_target="tpu_custom_call" | custom-call | flops 805306368 | bytes 9437184 | tf_op jit(solution)/shard_map/pallas_call | solution.py:324
  28.7 2.3 %shard_map.86 = (bf16[32,2048]{1,0:T(8,128)(2,1)}, f32[1,32]{1,0:T(1,128)}, bf16[1,3,2048,384]{3,2,1,0:T(8,128)(2,1)}) custom-call(bf16[256,512]{1,0:T(8,128)(2,1)S(1)} %get-tuple-element.10.got_d, bf16[128,256]{1,0:T(8,128)(2,1)S(1)} %get-tuple-element.11.back, f32[1,32]{1,0:T(1,128)S(1)} %get-tuple-element.12.d_prob, ...), custom_call_target="tpu_custom_call" | custom-call | tf_op jit(solution)/shard_map/pallas_call | solution.py:369

commit v3 on v2

--- a/solution.py
+++ b/solution.py
@@ -17,10 +17,6 @@
     return jnp.dot(a, b, preferred_element_type=F32)
 
 
-def dot_nt(a, b):
-    return lax.dot_general(a, b, (((1,), (1,)), ((), ())), preferred_element_type=F32)
-
-
 def dot_tn(a, b):
     return lax.dot_general(a, b, (((0,), (0,)), ((), ())), preferred_element_type=F32)
 
@@ -29,7 +25,7 @@
     n, blk, group,
     tok_hbm, go_hbm, prob_hbm, be_hbm, live_hbm, w_ref,
     got_d, back_ref, dprob_ref, wg_ref,
-    tok_ref, go_ref, prob_ref, be_ref, live_ref, wcat, wdown,
+    tok_ref, go_ref, prob_ref, be_ref, live_ref, wcat, wback, wdown,
     send_x, send_c, got_x, got_c, send_d, send_t, got_t, rows_x, rows_c, d_cat, hid,
     in_sem, w_sem, sx_sem, rx_sem, sc_sem, rc_sem, sd_sem, rd_sem, st_sem, rt_sem,
 ):
@@ -82,13 +78,6 @@
     def whole(first, last, src, dst, ssem, rsem):
         return remote(src, dst, ssem, rsem, ahead(1), first, last - first)
 
-    barrier = pltpu.get_barrier_semaphore()
-    slots(
-        1, n,
-        lambda k: pl.semaphore_signal(
-            barrier, inc=1, device_id={"expert": ahead(k)}, device_id_type=MESH
-        ),
-    )
     inputs = [
         pltpu.make_async_copy(src, dst, in_sem.at[j])
         for j, (src, dst) in enumerate(
@@ -98,7 +87,16 @@
             )
         )
     ]
-    for load in inputs:
+    for load in inputs[:3]:
+        load.start()
+    barrier = pltpu.get_barrier_semaphore()
+    slots(
+        1, n,
+        lambda k: pl.semaphore_signal(
+            barrier, inc=1, device_id={"expert": ahead(k)}, device_id_type=MESH
+        ),
+    )
+    for load in inputs[3:]:
         load.start()
     loads = [
         pltpu.make_async_copy(w_ref.at[0, 0], wcat.at[:, pl.ds(0, ff)], w_sem.at[0]),
@@ -210,34 +208,38 @@
 
         def forward(self):
             def body(first, slot_rows, here):
-                d_cat[here, :] = dot(rows_x[here, :], wcat[...])
+                both = dot(rows_x[here, :], wcat[...])
+                gate, up = both[:, :ff], both[:, ff:]
+                sigma = jax.nn.sigmoid(gate)
+                active = gate * sigma
+                hid[here, :] = (active * up).astype(BF16)
+                d_cat[here, :ff] = up * sigma * (1.0 + gate * (1.0 - sigma))
+                d_cat[here, ff:] = active
 
             self.each(body)
 
         def backward(self):
             def body(first, slot_rows, here):
-                gate, up = d_cat[here, :ff], d_cat[here, ff:]
                 pulled = dot(rows_c[here, :], wdown[...])
-                sigma = jax.nn.sigmoid(gate)
-                active = gate * sigma
-                hidden = (active * up).astype(BF16)
-                hid[here, :] = hidden
+                hidden = hid[here, :]
                 share = jnp.sum(hidden.astype(F32) * pulled, axis=1, keepdims=True)
                 share = jnp.broadcast_to(share, (self.grow, send_t.shape[2]))
                 for j in range(self.count):
                     send_t[first + j] = share[j * blk:(j + 1) * blk, :]
-                d_cat[here, :ff] = pulled * up * sigma * (1.0 + gate * (1.0 - sigma))
-                d_cat[here, ff:] = pulled * active
-                d_in = dot_nt(d_cat[here, :].astype(BF16), wcat[...]).astype(BF16)
+                d_both = jnp.concatenate([pulled, pulled], axis=1) * d_cat[here, :]
+                d_cat[here, :] = d_both
+                d_in = dot(d_both.astype(BF16), wback[...]).astype(BF16)
                 send_d[slot_rows, :] = dot(self.toslot, stacked(d_in)).astype(BF16)
 
             self.each(body)
 
     early, late = Chunk(0, mid, 3 * group), Chunk(mid, n, group)
+    for load in loads:
+        load.wait()
+    for p in range(parts):
+        wback[:, p * pw:(p + 1) * pw] = wcat[p * pw:(p + 1) * pw, :].T
     whole(1, mid, send_x, got_x, sx_sem.at[0], rx_sem.at[0]).wait_recv()
     early.unpack(got_x, rows_x)
-    for load in loads:
-        load.wait()
     early.forward()
     whole(1, mid, send_c, got_c, sc_sem.at[0], rc_sem.at[0]).wait_recv()
     early.unpack(got_c, rows_c)
@@ -337,6 +339,7 @@
             pltpu.SMEM(block_expert.shape, jnp.int32),
             pltpu.SMEM(block_live.shape, jnp.int32),
             pltpu.VMEM((width, 2 * ff), BF16),
+            pltpu.VMEM((2 * ff, width), BF16),
             pltpu.VMEM((width, ff), BF16),
             *[pltpu.VMEM(slots, BF16) for _ in range(5)],
             *[pltpu.VMEM((n, blk, 128), F32) for _ in range(2)],

time: 31.1 us -> 31.1 us (level)
  no operation moved by 1% of the time
where the time goes in v3:
time: 31.1 us; the launch traced here: 30.9 us
  Pallas kernels  30.3 us (97%)
  between operations  0.64 us (2%)
    pallas_call x1, Pallas kernels, shards(): pl.pallas_call(functools.partial(kernel, n, blk, group), out_shape=(pltpu...  28 us
    pallas_call x1, Pallas kernels, shards(): pl.pallas_call(store_kernel, out_shape=tuple((jax.ShapeDtypeStruct(*shape...  2.25 us

profile of v3, /device:TPU:0, one launch (start us, length us, event | category | flops | bytes accessed | tf_op | source)
XLA Modules:
  0.0 30.9 jit_solution(14989317796511682253)
XLA Ops:
  0.6 28.0 %shard_map.85 = (bf16[256,512]{1,0:T(8,128)(2,1)S(1)}, bf16[128,256]{1,0:T(8,128)(2,1)S(1)}, f32[1,32]{1,0:T(1,128)S(1)}, bf16[1,3,2048,384]{3,2,1,0:T(8,128)(2,1)S(1)}) custom-call(bf16[32,2048]{1,0:T(8,128)(2,1)} %tok_hbm.1, bf16[32,2048]{1,0:T(8,128)(2,1)} %go_hbm.1, f32[1,32]{1,0:T(1,128)} %bitcast.2, s32[8]{0:T(128)} %be_hbm.1, s32[8]{0:T(128)} %live_hbm.1, ...), custom_call_target="tpu_custom_call" | custom-call | flops 805306368 | bytes 9437184 | tf_op jit(solution)/shard_map/pallas_call | solution.py:326
  28.6 2.3 %shard_map.86 = (bf16[32,2048]{1,0:T(8,128)(2,1)}, f32[1,32]{1,0:T(1,128)}, bf16[1,3,2048,384]{3,2,1,0:T(8,128)(2,1)}) custom-call(bf16[256,512]{1,0:T(8,128)(2,1)S(1)} %get-tuple-element.10.got_d, bf16[128,256]{1,0:T(8,128)(2,1)S(1)} %get-tuple-element.11.back, f32[1,32]{1,0:T(1,128)S(1)} %get-tuple-element.12.d_prob, ...), custom_call_target="tpu_custom_call" | custom-call | tf_op jit(solution)/shard_map/pallas_call | solution.py:372

commit v4 on v3

--- a/solution.py
+++ b/solution.py
@@ -223,9 +223,14 @@
                 pulled = dot(rows_c[here, :], wdown[...])
                 hidden = hid[here, :]
                 share = jnp.sum(hidden.astype(F32) * pulled, axis=1, keepdims=True)
-                share = jnp.broadcast_to(share, (self.grow, send_t.shape[2]))
+                wide = (self.grow, send_t.shape[2])
+                lane = lax.broadcasted_iota(jnp.int32, wide, 1)
+                row = lax.broadcasted_iota(jnp.int32, wide, 0)
+                share = jnp.where(lane % blk == row % blk, jnp.broadcast_to(share, wide), 0.0)
                 for j in range(self.count):
-                    send_t[first + j] = share[j * blk:(j + 1) * blk, :]
+                    send_t[first + j] = jnp.sum(
+                        share[j * blk:(j + 1) * blk, :], axis=0, keepdims=True
+                    )
                 d_both = jnp.concatenate([pulled, pulled], axis=1) * d_cat[here, :]
                 d_cat[here, :] = d_both
                 d_in = dot(d_both.astype(BF16), wback[...]).astype(BF16)
@@ -247,14 +252,15 @@
     send(1, half, send_d, got_d, sd_sem, rd_sem, behind)
     got_d[:SLOT, :] = send_d[:SLOT, :]
     whole(mid, n, send_x, got_x, sx_sem.at[1], rx_sem.at[1]).wait_recv()
+    send(half, mid, send_d, got_d, sd_sem, rd_sem, behind)
+    send(1, mid, send_t, got_t, st_sem, rt_sem, behind)
     late.unpack(got_x, rows_x)
     late.forward()
     whole(mid, n, send_c, got_c, sc_sem.at[1], rc_sem.at[1]).wait_recv()
-    send(half, mid, send_d, got_d, sd_sem, rd_sem, behind)
     late.unpack(got_c, rows_c)
     late.backward()
     send(mid, n, send_d, got_d, sd_sem, rd_sem, behind)
-    send(1, n, send_t, got_t, st_sem, rt_sem, behind)
+    send(mid, n, send_t, got_t, st_sem, rt_sem, behind)
     got_t[0] = send_t[0]
 
     d_all = d_cat[...].astype(BF16)
@@ -267,15 +273,13 @@
 
     every_t = whole(1, n, send_t, got_t, st_sem, rt_sem)
     every_t.wait_recv()
-    lane = lax.broadcasted_iota(jnp.int32, (blk, got_t.shape[2]), 1)
-    row = lax.broadcasted_iota(jnp.int32, (blk, got_t.shape[2]), 0)
+    lane = lax.broadcasted_iota(jnp.int32, (1, got_t.shape[2]), 1)
     per = lanes // blk
     for g in range(rows // lanes):
-        line = jnp.zeros((blk, got_t.shape[2]), F32)
+        line = jnp.zeros((1, got_t.shape[2]), F32)
         for j in range(per):
-            line = jnp.where(lane == j * blk + row, got_t[slot_of(be_ref[g * per + j])], line)
-        total = jnp.sum(line, axis=0, keepdims=True)[:, :lanes]
-        dprob_ref[g:g + 1, :] = total / prob_ref[g:g + 1, :]
+            line = jnp.where(lane // blk == j, got_t[slot_of(be_ref[g * per + j])], line)
+        dprob_ref[g:g + 1, :] = line[:, :lanes] / prob_ref[g:g + 1, :]
 
     for j, (first, last) in enumerate(((1, mid), (mid, n))):
         whole(first, last, send_x, got_x, sx_sem.at[j], rx_sem.at[j]).wait_send()
@@ -342,7 +346,7 @@
             pltpu.VMEM((2 * ff, width), BF16),
             pltpu.VMEM((width, ff), BF16),
             *[pltpu.VMEM(slots, BF16) for _ in range(5)],
-            *[pltpu.VMEM((n, blk, 128), F32) for _ in range(2)],
+            *[pltpu.VMEM((n, 1, 128), F32) for _ in range(2)],
             pltpu.VMEM((every, width), BF16),
             pltpu.VMEM((every, width), BF16),
             pltpu.VMEM((every, 2 * ff), F32),

time: 31.1 us -> 28.7 us (0.923)
  Pallas kernels: 30.3 us -> 27.9 us
    pallas_call x1, Pallas kernels: 28 us -> 25.7 us  [shards(): pl.pallas_call(functools.partial(kernel, n, blk, group), out_shape=(pltpu...]
where the time goes in v4:
time: 28.7 us; the launch traced here: 28.6 us
  Pallas kernels  27.9 us (97%)
  between operations  0.64 us (2%)
    pallas_call x1, Pallas kernels, shards(): pl.pallas_call(functools.partial(kernel, n, blk, group), out_shape=(pltpu...  25.7 us
    pallas_call x1, Pallas kernels, shards(): pl.pallas_call(store_kernel, out_shape=tuple((jax.ShapeDtypeStruct(*shape...  2.25 us

profile of v4, /device:TPU:0, one launch (start us, length us, event | category | flops | bytes accessed | tf_op | source)
XLA Modules:
  0.0 28.6 jit_solution(15674520901860775766)
XLA Ops:
  0.6 25.7 %shard_map.85 = (bf16[256,512]{1,0:T(8,128)(2,1)S(1)}, bf16[128,256]{1,0:T(8,128)(2,1)S(1)}, f32[1,32]{1,0:T(1,128)S(1)}, bf16[1,3,2048,384]{3,2,1,0:T(8,128)(2,1)S(1)}) custom-call(bf16[32,2048]{1,0:T(8,128)(2,1)} %tok_hbm.1, bf16[32,2048]{1,0:T(8,128)(2,1)} %go_hbm.1, f32[1,32]{1,0:T(1,128)} %bitcast.2, s32[8]{0:T(128)} %be_hbm.1, s32[8]{0:T(128)} %live_hbm.1, ...), custom_call_target="tpu_custom_call" | custom-call | flops 805306368 | bytes 9437184 | tf_op jit(solution)/shard_map/pallas_call | solution.py:330
  26.3 2.3 %shard_map.86 = (bf16[32,2048]{1,0:T(8,128)(2,1)}, f32[1,32]{1,0:T(1,128)}, bf16[1,3,2048,384]{3,2,1,0:T(8,128)(2,1)}) custom-call(bf16[256,512]{1,0:T(8,128)(2,1)S(1)} %get-tuple-element.10.got_d, bf16[128,256]{1,0:T(8,128)(2,1)S(1)} %get-tuple-element.11.back, f32[1,32]{1,0:T(1,128)S(1)} %get-tuple-element.12.d_prob, ...), custom_call_target="tpu_custom_call" | custom-call | tf_op jit(solution)/shard_map/pallas_call | solution.py:376

commit v5 on v4

--- a/solution.py
+++ b/solution.py
@@ -42,20 +42,27 @@
     side = me // half * half
     place = me % half
 
+    def base(k):
+        if isinstance(k, int):
+            return side if k < half else half - side
+        return jnp.where(k < half, side, half - side)
+
     def ahead(k):
-        base = jnp.where(k < half, side, half - side)
-        return base + (place + k) % half
+        return base(k) + (place + k) % half
 
     def behind(k):
-        base = jnp.where(k < half, side, half - side)
-        return base + (place - k + n) % half
+        return base(k) + (place - k + n) % half
 
     def slots(first, last, body):
         def step(k, carry):
             body(k)
             return carry
 
-        lax.fori_loop(first, last, step, 0)
+        if last - first <= 16:
+            for k in range(first, last):
+                body(k)
+        else:
+            lax.fori_loop(first, last, step, 0)
 
     def part_of(ref, first, count):
         if len(ref.shape) == 3:
@@ -249,11 +256,11 @@
     whole(1, mid, send_c, got_c, sc_sem.at[0], rc_sem.at[0]).wait_recv()
     early.unpack(got_c, rows_c)
     early.backward()
+    send(half, mid, send_d, got_d, sd_sem, rd_sem, behind)
     send(1, half, send_d, got_d, sd_sem, rd_sem, behind)
+    send(1, mid, send_t, got_t, st_sem, rt_sem, behind)
     got_d[:SLOT, :] = send_d[:SLOT, :]
     whole(mid, n, send_x, got_x, sx_sem.at[1], rx_sem.at[1]).wait_recv()
-    send(half, mid, send_d, got_d, sd_sem, rd_sem, behind)
-    send(1, mid, send_t, got_t, st_sem, rt_sem, behind)
     late.unpack(got_x, rows_x)
     late.forward()
     whole(mid, n, send_c, got_c, sc_sem.at[1], rc_sem.at[1]).wait_recv()

time: 28.7 us -> 29.6 us (1.031)
  Pallas kernels: 27.9 us -> 28.8 us
    pallas_call x1, Pallas kernels: 25.7 us -> 26.6 us  [shards(): pl.pallas_call(functools.partial(kernel, n, blk, group), out_shape=(pltpu...]
where the time goes in v5:
time: 29.6 us; the launch traced here: 29.5 us
  Pallas kernels  28.8 us (97%)
  between operations  0.64 us (2%)
    pallas_call x1, Pallas kernels, shards(): pl.pallas_call(functools.partial(kernel, n, blk, group), out_shape=(pltpu...  26.6 us
    pallas_call x1, Pallas kernels, shards(): pl.pallas_call(store_kernel, out_shape=tuple((jax.ShapeDtypeStruct(*shape...  2.25 us

profile of v5, /device:TPU:0, one launch (start us, length us, event | category | flops | bytes accessed | tf_op | source)
XLA Modules:
  0.0 29.5 jit_solution(17682791421247340684)
XLA Ops:
  0.6 26.6 %shard_map.85 = (bf16[256,512]{1,0:T(8,128)(2,1)S(1)}, bf16[128,256]{1,0:T(8,128)(2,1)S(1)}, f32[1,32]{1,0:T(1,128)S(1)}, bf16[1,3,2048,384]{3,2,1,0:T(8,128)(2,1)S(1)}) custom-call(bf16[32,2048]{1,0:T(8,128)(2,1)} %tok_hbm.1, bf16[32,2048]{1,0:T(8,128)(2,1)} %go_hbm.1, f32[1,32]{1,0:T(1,128)} %bitcast.2, s32[8]{0:T(128)} %be_hbm.1, s32[8]{0:T(128)} %live_hbm.1, ...), custom_call_target="tpu_custom_call" | custom-call | flops 805306368 | bytes 9437184 | tf_op jit(solution)/shard_map/pallas_call | solution.py:337
  27.2 2.3 %shard_map.86 = (bf16[32,2048]{1,0:T(8,128)(2,1)}, f32[1,32]{1,0:T(1,128)}, bf16[1,3,2048,384]{3,2,1,0:T(8,128)(2,1)}) custom-call(bf16[256,512]{1,0:T(8,128)(2,1)S(1)} %get-tuple-element.10.got_d, bf16[128,256]{1,0:T(8,128)(2,1)S(1)} %get-tuple-element.11.back, f32[1,32]{1,0:T(1,128)S(1)} %get-tuple-element.12.d_prob, ...), custom_call_target="tpu_custom_call" | custom-call | tf_op jit(solution)/shard_map/pallas_call | solution.py:383

commit v6 on v5

--- a/solution.py
+++ b/solution.py
@@ -137,21 +137,25 @@
 
     bulk = min(n, 16) * SLOT
 
-    def pack(value, into):
+    few = group * SLOT
+
+    def pack(first, last, value, into):
         def step(c, carry):
-            at = pl.multiple_of(c * bulk, bulk)
-            ids = lax.broadcasted_iota(jnp.int32, (bulk, cols), 0) + c * bulk
-            into[pl.ds(at, bulk), :] = dot(one_hot(ids == key_row), value).astype(BF16)
+            at = pl.multiple_of(first * SLOT + c * few, SLOT)
+            ids = lax.broadcasted_iota(jnp.int32, (few, cols), 0) + at
+            into[pl.ds(at, few), :] = dot(one_hot(ids == key_row), value).astype(BF16)
             return carry
 
-        lax.fori_loop(0, n * SLOT // bulk, step, 0)
+        lax.fori_loop(0, (last - first) // group, step, 0)
 
     for load in inputs[:3]:
         load.wait()
     key_row = keys((1, cols), 1)
-    pack(stacked(tok_ref[...]), send_x)
+    tok4 = stacked(tok_ref[...])
+    pack(half, mid, tok4, send_x)
     pl.semaphore_wait(barrier, n - 1)
     send(half, mid, send_x, got_x, sx_sem.at[0], rx_sem.at[0], ahead)
+    pack(0, half, tok4, send_x)
     send(1, half, send_x, got_x, sx_sem.at[0], rx_sem.at[0], ahead)
 
     for load in inputs[3:]:
@@ -165,10 +169,14 @@
         line = jnp.broadcast_to(prob_ref[g:g + 1, :], square)
         probs.append(jnp.sum(jnp.where(diagonal, line, 0.0), axis=1, keepdims=True))
     prob = jnp.concatenate(probs, axis=0) if len(probs) > 1 else probs[0]
-    pack(stacked((prob * go_ref[...].astype(F32)).astype(BF16)), send_c)
+    cot4 = stacked((prob * go_ref[...].astype(F32)).astype(BF16))
+    pack(half, mid, cot4, send_c)
     send(half, mid, send_c, got_c, sc_sem.at[0], rc_sem.at[0], ahead)
+    pack(0, half, cot4, send_c)
     send(1, half, send_c, got_c, sc_sem.at[0], rc_sem.at[0], ahead)
+    pack(mid, n, tok4, send_x)
     send(mid, n, send_x, got_x, sx_sem.at[1], rx_sem.at[1], ahead)
+    pack(mid, n, cot4, send_c)
     send(mid, n, send_c, got_c, sc_sem.at[1], rc_sem.at[1], ahead)
     got_x[:SLOT, :] = send_x[:SLOT, :]
     got_c[:SLOT, :] = send_c[:SLOT, :]
@@ -256,11 +264,11 @@
     whole(1, mid, send_c, got_c, sc_sem.at[0], rc_sem.at[0]).wait_recv()
     early.unpack(got_c, rows_c)
     early.backward()
-    send(half, mid, send_d, got_d, sd_sem, rd_sem, behind)
     send(1, half, send_d, got_d, sd_sem, rd_sem, behind)
-    send(1, mid, send_t, got_t, st_sem, rt_sem, behind)
     got_d[:SLOT, :] = send_d[:SLOT, :]
     whole(mid, n, send_x, got_x, sx_sem.at[1], rx_sem.at[1]).wait_recv()
+    send(half, mid, send_d, got_d, sd_sem, rd_sem, behind)
+    send(1, mid, send_t, got_t, st_sem, rt_sem, behind)
     late.unpack(got_x, rows_x)
     late.forward()
     whole(mid, n, send_c, got_c, sc_sem.at[1], rc_sem.at[1]).wait_recv()
@@ -298,22 +306,29 @@
 
 
 def store_kernel(got_d, back, d_prob, wg, dtok_hbm, dprob_hbm, wg_hbm, d_tokens, sem):
+    cut = wg.shape[2] // 2
     stores = [
-        pltpu.make_async_copy(wg, wg_hbm, sem.at[0]),
-        pltpu.make_async_copy(d_prob, dprob_hbm, sem.at[1]),
-        pltpu.make_async_copy(d_tokens, dtok_hbm, sem.at[2]),
+        pltpu.make_async_copy(
+            wg.at[0, j, pl.ds(h * cut, cut)], wg_hbm.at[0, j, pl.ds(h * cut, cut)],
+            sem.at[2 * j + h],
+        )
+        for j in range(3)
+        for h in range(2)
     ]
-    stores[0].start()
-    stores[1].start()
+    stores.append(pltpu.make_async_copy(d_prob, dprob_hbm, sem.at[6]))
+    last = pltpu.make_async_copy(d_tokens, dtok_hbm, sem.at[7])
+    for store in stores:
+        store.start()
     rows = d_tokens.shape[0]
     pw = got_d.shape[1]
     parts = d_tokens.shape[1] // pw
     for p in range(parts):
         picked = dot(back[p * rows:(p + 1) * rows, :], got_d[...])
         d_tokens[:, p * pw:(p + 1) * pw] = picked.astype(BF16)
-    stores[2].start()
+    last.start()
     for store in stores:
         store.wait()
+    last.wait()
 
 
 def shards(n, tokens, grad_out, route_prob, block_expert, block_live, expert_weights):
@@ -385,7 +400,7 @@
         out_shape=tuple(jax.ShapeDtypeStruct(*shape) for shape in shapes),
         in_specs=[vmem] * 4,
         out_specs=(any_,) * 3,
-        scratch_shapes=[pltpu.VMEM((rows, width), BF16), dma((3,))],
+        scratch_shapes=[pltpu.VMEM((rows, width), BF16), dma((8,))],
         compiler_params=pltpu.CompilerParams(vmem_limit_bytes=8 * 1024 * 1024),
     )(*results)
     return (d_tokens, d_prob.reshape(rows), weight_grads)

time: 29.6 us -> 28.5 us (0.963)
  Pallas kernels: 28.8 us -> 27.7 us
    pallas_call x1, Pallas kernels: 26.6 us -> 25.5 us  [shards(): pl.pallas_call(functools.partial(kernel, n, blk, group), out_shape=(pltpu...]
where the time goes in v6:
time: 28.5 us; the launch traced here: 28.4 us
  Pallas kernels  27.7 us (97%)
  between operations  0.64 us (2%)
    pallas_call x1, Pallas kernels, shards(): pl.pallas_call(functools.partial(kernel, n, blk, group), out_shape=(pltpu...  25.5 us
    pallas_call x1, Pallas kernels, shards(): pl.pallas_call(store_kernel, out_shape=tuple((jax.ShapeDtypeStruct(*shape...  2.29 us

profile of v6, /device:TPU:0, one launch (start us, length us, event | category | flops | bytes accessed | tf_op | source)
XLA Modules:
  0.0 28.4 jit_solution(8031371251290480116)
XLA Ops:
  0.6 25.5 %shard_map.85 = (bf16[256,512]{1,0:T(8,128)(2,1)S(1)}, bf16[128,256]{1,0:T(8,128)(2,1)S(1)}, f32[1,32]{1,0:T(1,128)S(1)}, bf16[1,3,2048,384]{3,2,1,0:T(8,128)(2,1)S(1)}) custom-call(bf16[32,2048]{1,0:T(8,128)(2,1)} %tok_hbm.1, bf16[32,2048]{1,0:T(8,128)(2,1)} %go_hbm.1, f32[1,32]{1,0:T(1,128)} %bitcast.2, s32[8]{0:T(128)} %be_hbm.1, s32[8]{0:T(128)} %live_hbm.1, ...), custom_call_target="tpu_custom_call" | custom-call | flops 805306368 | bytes 9437184 | tf_op jit(solution)/shard_map/pallas_call | solution.py:352
  26.1 2.3 %shard_map.86 = (bf16[32,2048]{1,0:T(8,128)(2,1)}, f32[1,32]{1,0:T(1,128)}, bf16[1,3,2048,384]{3,2,1,0:T(8,128)(2,1)}) custom-call(bf16[256,512]{1,0:T(8,128)(2,1)S(1)} %get-tuple-element.10.got_d, bf16[128,256]{1,0:T(8,128)(2,1)S(1)} %get-tuple-element.11.back, f32[1,32]{1,0:T(1,128)S(1)} %get-tuple-element.12.d_prob, ...), custom_call_target="tpu_custom_call" | custom-call | tf_op jit(solution)/shard_map/pallas_call | solution.py:398
